TPU v7x, 32 devices: a whole 2x2x4 slice. The times are simulated.
32 devices in a mesh: groups: 2 (over x), row: 16 (over z, y, core).
Axes of the slice: x: 2, y: 2, z: 4, core: 2. Of those that a mesh axis runs over, the one named last changes fastest.
Arguments:
- pair: bfloat16 [320, 160, 128], P(('groups', 'row')), parts along dimension 0, may hold values from -6 to 6
- mask: int32 [320], P('groups'), parts along dimension 0, may hold values 0 or 1
- chain: int32 [320], P('groups'), parts along dimension 0, may hold values from 0 to 5, never falling along the last dimension, each value on 1 to 53 neighbouring positions
- tri_proj: bfloat16 [128, 512], replicated, may hold values from -0.5 to 0.5
- tri_gate: bfloat16 [128, 128], replicated, may hold values from -0.5 to 0.5
- tri_out: bfloat16 [128, 128], replicated, may hold values from -0.5 to 0.5
- att_proj: bfloat16 [128, 512], replicated, may hold values from -0.5 to 0.5
- att_bias: float32 [128, 4], replicated, may hold values from -23.864854 to 23.864854
- same_chain: float32 [4], replicated, may hold values from -2 to 2
- att_out: bfloat16 [128, 128], replicated, may hold values from -0.26367188 to 0.26367188
Outputs:
- updated: bfloat16 [320, 160, 128], P(('groups', 'row')), parts along dimension 0
There are 2 independent parts, one for each index of `groups`. A program takes and returns all parts, laid end to end along the dimension named above; an argument that names none is the same for every part. Nothing has to cross between parts.
Inputs may be any that keep to these rules, and one draw needn't show every extreme that they name: `mask`: 1 marks a resolved token, 0 a missing one. chain number of each token; each chain is one contiguous run of at most 53 tokens, numbers never falling along the tokens.
All inputs are finite; a program needn't handle non-finite values.
Results may differ from a plain program's by a relative error of at most 0.013.
Values may be sent and summed in bfloat16 or wider, within the bound.
A program may use at most 128 MiB of HBM per device.

v0:
```python
import jax
import jax.numpy as jnp
from jax import lax
from jax.sharding import PartitionSpec as P


def layer_norm(values):
    centre_mean = jnp.mean(values, axis=-1, keepdims=True)
    centred = values - centre_mean
    spread = jnp.mean(centred * centred, axis=-1, keepdims=True)
    return centred * lax.rsqrt(spread + 1e-05)


def chain_logits(bias_block, same_chain, chain_rows, chain, mask_float):
    same = (chain_rows[:, None] == chain[None, :]).astype(jnp.float32)
    logit_bias = bias_block.astype(jnp.float32) + same_chain[:, None, None] * same[None, :, :]
    return logit_bias + 10000.0 * (mask_float - 1.0)[None, None, :]


def attend(query, att_gate, key, value, logit_bias, head_count, head_size):
    block_len = query.shape[1]
    tokens = key.shape[1]
    width = head_count * head_size

    def one_row(inputs):
        query_row, key_row, value_row, gate_row = inputs
        query_heads = query_row.reshape(block_len, head_count, head_size)
        key_heads = key_row.reshape(tokens, head_count, head_size)
        value_heads = value_row.reshape(tokens, head_count, head_size)
        scores = (
            jnp.einsum("jhd,khd->hjk", query_heads, key_heads, preferred_element_type=jnp.float32)
            + logit_bias
        )
        row_max = jnp.max(scores, axis=2, keepdims=True)
        exp_scores = jnp.exp(scores - row_max)
        weight = (exp_scores / jnp.sum(exp_scores, axis=2, keepdims=True)).astype(jnp.bfloat16)
        mixed_heads = jnp.einsum(
            "hjk,khd->jhd", weight, value_heads, preferred_element_type=jnp.float32
        )
        return (gate_row * mixed_heads.reshape(block_len, width)).astype(jnp.bfloat16)

    return lax.map(one_row, (query, key, value, att_gate))


def per_device(
    pair, mask, chain, tri_proj, tri_gate, tri_out, att_proj, att_bias, same_chain, att_out
):
    local_rows, tokens, width = pair.shape
    head_count = same_chain.shape[0]
    head_size = width // head_count
    scale = head_size ** (-0.5)
    part_count = lax.axis_size("row")
    share_width = width // part_count
    first_row = lax.axis_index("row") * local_rows
    mask_float = mask.astype(jnp.float32)
    row_mask = lax.dynamic_slice_in_dim(mask_float, first_row, local_rows)

    def project_row(inputs):
        pair_row, mask_value = inputs
        normed = layer_norm(pair_row.astype(jnp.float32)).astype(jnp.bfloat16)
        projected = jnp.dot(normed, tri_proj, preferred_element_type=jnp.float32)
        weight = (mask_value * mask_float)[:, None]
        left_proj = (
            weight * jax.nn.sigmoid(projected[:, 2 * width : 3 * width]) * projected[:, :width]
        ).astype(jnp.bfloat16)
        right_proj = (
            weight * jax.nn.sigmoid(projected[:, 3 * width :]) * projected[:, width : 2 * width]
        ).astype(jnp.bfloat16)
        out_gate = jax.nn.sigmoid(jnp.dot(normed, tri_gate, preferred_element_type=jnp.float32))
        return (left_proj, right_proj, out_gate)

    left_proj, right_proj, out_gate = lax.map(project_row, (pair, row_mask))
    left_lay = jnp.transpose(left_proj, (2, 0, 1)).reshape(
        part_count, share_width, local_rows, tokens
    )
    right_lay = jnp.transpose(right_proj, (2, 0, 1)).reshape(
        part_count, share_width, local_rows, tokens
    )
    got_left, got_right = (
        lax.all_to_all(left_lay, "row", split_axis=0, concat_axis=2, tiled=True),
        lax.all_to_all(right_lay, "row", split_axis=0, concat_axis=2, tiled=True),
    )
    product = jnp.einsum(
        "cik,cjk->cij", got_left[0], got_right[0], preferred_element_type=jnp.float32
    )
    returned = lax.all_to_all(
        product.astype(jnp.bfloat16)[None], "row", split_axis=2, concat_axis=0, tiled=True
    )
    tri_sum = jnp.transpose(returned.reshape(width, local_rows, tokens), (1, 2, 0))

    def finish_row(inputs):
        pair_row, summed, gate_row = inputs
        tri_norm = layer_norm(summed.astype(jnp.float32)).astype(jnp.bfloat16)
        update = jnp.dot(tri_norm, tri_out, preferred_element_type=jnp.float32)
        mid_pair = (pair_row.astype(jnp.float32) + gate_row * update).astype(jnp.bfloat16)
        mid_norm = layer_norm(mid_pair.astype(jnp.float32)).astype(jnp.bfloat16)
        att_all = jnp.dot(mid_norm, att_proj, preferred_element_type=jnp.float32)
        query = (att_all[:, :width] * scale).astype(jnp.bfloat16)
        key = att_all[:, width : 2 * width].astype(jnp.bfloat16)
        value = att_all[:, 2 * width : 3 * width].astype(jnp.bfloat16)
        att_gate = jax.nn.sigmoid(att_all[:, 3 * width :])
        pair_bias = jnp.dot(mid_norm, att_bias, preferred_element_type=jnp.float32).astype(
            jnp.bfloat16
        )
        return (mid_pair, query, key, value, att_gate, pair_bias)

    mid_pair, query, key, value, att_gate, pair_bias = lax.map(
        finish_row, (pair, tri_sum, out_gate)
    )
    bias_lay = jnp.transpose(pair_bias, (2, 0, 1))
    full_bias = lax.all_gather(bias_lay, "row", axis=1, tiled=True)
    logit_bias = chain_logits(full_bias, same_chain, chain, chain, mask_float)
    gated = attend(query, att_gate, key, value, logit_bias, head_count, head_size)
    projected_out = jnp.dot(gated.reshape(-1, width), att_out, preferred_element_type=jnp.float32)
    return (mid_pair.astype(jnp.float32) + projected_out.reshape(local_rows, tokens, width)).astype(
        jnp.bfloat16
    )


def solution(mesh):
    return jax.shard_map(
        per_device,
        mesh=mesh,
        in_specs=(
            P(("groups", "row"), None, None),
            P("groups"),
            P("groups"),
            P(),
            P(),
            P(),
            P(),
            P(),
            P(),
            P(),
        ),
        out_specs=P(("groups", "row"), None, None),
        check_vma=False,
    )
```

profile of v0, /device:TPU:0, one launch (start us, length us, event | category | flops | bytes accessed | tf_op | source)
XLA Modules:
  0.0 171.8 jit_solution(10399179585263291489)
XLA Ops:
  1.8 21.9 %while.44 = (s32[]{:T(128)}, bf16[10,160,128]{2,1,0:T(8,128)(2,1)S(1)}, bf16[10,160,128]{2,1,0:T(8,128)(2,1)S(1)}, f32[10,160,128]{2,1,0:T(8,128)S(1)}, f32[10]{...) while((s32[]{:T(128)}, ...), condition=%wide.region_3.4_spmd, body=%wide.region_0.3_spmd.sunk | while | flops 26808640 | bytes 1158917 | solution.py:72
  24.8 0.9 copy.53
  25.6 7.5 %all-to-all-start = ((bf16[16,8,10,160]{3,1,2,0:T(8,128)(2,1)}), bf16[16,8,10,160]{3,1,2,0:T(8,128)(2,1)S(1)}, u32[]{:S(2)}, u32[]{:S(2)}) async-start(bf16[16,8,10,160]{3,1,2,0:T(8,128)(2,1)} %copy.53), calls=%async_computation | async-start | bytes 1310720 | tf_op jit(solution)/shard_map/all_to_all | solution.py:80
  33.5 16.3 %all-to-all-done = bf16[16,8,10,160]{3,1,2,0:T(8,128)(2,1)S(1)} async-done(((bf16[16,8,10,160]{3,1,2,0:T(8,128)(2,1)}), bf16[16,8,10,160]{3,1,2,0:T(8,128)(2,1)S(1)}, u32[]{:S(2)}, u32[]{:S(2)}) %all-to-all-start) | async-done | bytes 409632 | tf_op jit(solution)/shard_map/all_to_all | solution.py:80
  49.8 22.8 %all_to_all.45 = bf16[16,8,10,160]{3,1,2,0:T(8,128)(2,1)S(1)} all-to-all(bf16[16,8,10,160]{3,1,2,0:T(8,128)(2,1)S(1)} %copy.55), channel_id=1, replica_groups=mesh['groups'=2,'row'=16] {'row'}, dimensions={0} | all-to-all | bytes 819200 | tf_op jit(solution)/shard_map/all_to_all | solution.py:81
  72.9 1.2 copy.58
  74.1 3.7 %all-to-all-start.2 = ((bf16[1,8,160,160]{3,1,0,2:T(8,128)(2,1)}), bf16[1,8,160,160]{3,1,0,2:T(8,128)(2,1)S(1)}, u32[]{:S(2)}, u32[]{:S(2)}) async-start(bf16[1,8,160,160]{3,1,0,2:T(8,128)(2,1)} %copy.58), calls=%async_computation.2 | async-start | bytes 1310720 | tf_op jit(solution)/shard_map/all_to_all | solution.py:86
  79.8 14.6 %all-to-all-done.2 = bf16[1,8,160,160]{3,1,0,2:T(8,128)(2,1)S(1)} async-done(((bf16[1,8,160,160]{3,1,0,2:T(8,128)(2,1)}), bf16[1,8,160,160]{3,1,0,2:T(8,128)(2,1)S(1)}, u32[]{:S(2)}, u32[]{:S(2)}) %all-to-all-start.2) | async-done | bytes 409632 | tf_op jit(solution)/shard_map/all_to_all | solution.py:86
  95.0 0.8 broadcast.109.clone2.1
  95.8 0.8 broadcast.109.clone2.2
  96.7 21.1 %while.45 = (s32[]{:T(128)}, bf16[10,160,128]{2,1,0:T(8,128)(2,1)S(1)}, bf16[10,160,128]{2,1,0:T(8,128)(2,1)S(1)}, bf16[10,160,128]{2,1,0:T(8,128)(2,1)}, bf16[1...) while((s32[]{:T(128)}, ...), condition=%wide.region_9.10_spmd, body=%wide.region_4.9_spmd.sunk | while | flops 27136320 | bytes 1616533 | solution.py:107
  118.7 21.3 %all_gather.3 = bf16[4,160,160]{2,0,1:T(4,128)(2,1)S(1)} all-gather(bf16[4,10,160]{2,0,1:T(4,128)(2,1)S(1)} %bitcast.174), channel_id=1, replica_groups=mesh['groups'=2,'row'=16] {'row'}, dimensions={1}, use_global_device_ids=true | all-gather | bytes 217600 | tf_op jit(solution)/shard_map/all_gather | solution.py:111
  140.0 1.1 add_add_fusion
  142.2 28.4 %while.46 = (s32[]{:T(128)}, bf16[10,160,128]{1,2,0:T(8,128)(2,1)S(1)}, f32[10,160,128]{2,1,0:T(8,128)S(1)}, bf16[10,160,128]{2,1,0:T(8,128)(2,1)}, bf16[10,160,...) while((s32[]{:T(128)}, ...), condition=%wide.region_13.14_spmd, body=%wide.region_10.13_spmd.sunk | while | flops 13763520 | bytes 2995301 | solution.py:42
  142.2 0.9 constant_dynamic-slice_fusion.9
  143.8 0.8 constant_dynamic-slice_fusion.8
  145.1 0.8 constant_dynamic-slice_fusion.9
  146.6 0.8 constant_dynamic-slice_fusion.8
  147.9 0.8 constant_dynamic-slice_fusion.9
  149.4 0.8 constant_dynamic-slice_fusion.8
  150.8 0.8 constant_dynamic-slice_fusion.9
  152.3 0.8 constant_dynamic-slice_fusion.8
  153.6 0.8 constant_dynamic-slice_fusion.9
  155.1 0.8 constant_dynamic-slice_fusion.8
  156.4 0.8 constant_dynamic-slice_fusion.9
  158.0 0.8 constant_dynamic-slice_fusion.8
  159.3 0.8 constant_dynamic-slice_fusion.9
  160.8 0.8 constant_dynamic-slice_fusion.8
  162.1 0.8 constant_dynamic-slice_fusion.9
  165.0 0.8 constant_dynamic-slice_fusion.9
  167.8 0.8 constant_dynamic-slice_fusion.9
  170.7 1.1 fusion.61
  (371 shorter events, 64.0 us)
Async XLA Ops:
  0.0 170.6 %copy-start = (bf16[128,128]{1,0:T(8,128)(2,1)S(1)}, bf16[128,128]{1,0:T(8,128)(2,1)}, u32[]{:S(2)}) copy-start(bf16[128,128]{1,0:T(8,128)(2,1)} %param.25) | copy-start | bytes 98308
  0.8 0.9 copy-start.1
  0.8 1.1 copy-start.3
  0.8 1.1 copy-start.18
  23.7 0.8 copy-start.6
  25.6 7.5 %copy-start.7 = (bf16[10,160,128]{2,1,0:T(8,128)(2,1)S(1)}, bf16[10,160,128]{2,1,0:T(8,128)(2,1)}, u32[]{:S(2)}) copy-start(bf16[10,160,128]{2,1,0:T(8,128)(2,1)} %copy-done.6) | copy-start | bytes 1228804
  25.6 24.1 %all-to-all-start = ((bf16[16,8,10,160]{3,1,2,0:T(8,128)(2,1)}), bf16[16,8,10,160]{3,1,2,0:T(8,128)(2,1)S(1)}, u32[]{:S(2)}, u32[]{:S(2)}) async-start(bf16[16,8,10,160]{3,1,2,0:T(8,128)(2,1)} %copy.53), calls=%async_computation | async-start | bytes 1310720 | tf_op jit(solution)/shard_map/all_to_all | solution.py:80
  74.1 3.8 %copy-start.15 = (f32[128,4]{0,1:T(4,128)S(1)}, f32[128,4]{0,1:T(4,128)}, u32[]{:S(2)}) copy-start(f32[128,4]{0,1:T(4,128)} %param.23) | copy-start | bytes 6148
  74.1 4.3 %copy-start.13 = (s32[160]{0:T(256)S(1)}, s32[160]{0:T(256)}, u32[]{:S(2)}) copy-start(s32[160]{0:T(256)} %param.17) | copy-start | bytes 1924
  74.1 4.9 %copy-start.14 = (s32[160]{0:T(256)S(1)}, s32[160]{0:T(256)}, u32[]{:S(2)}) copy-start(s32[160]{0:T(256)} %param.18) | copy-start | bytes 1924
  74.1 20.3 %all-to-all-start.2 = ((bf16[1,8,160,160]{3,1,0,2:T(8,128)(2,1)}), bf16[1,8,160,160]{3,1,0,2:T(8,128)(2,1)S(1)}, u32[]{:S(2)}, u32[]{:S(2)}) async-start(bf16[1,8,160,160]{3,1,0,2:T(8,128)(2,1)} %copy.58), calls=%async_computation.2 | async-start | bytes 1310720 | tf_op jit(solution)/shard_map/all_to_all | solution.py:86
  94.9 1.8 %copy-start.2 = (bf16[128,512]{1,0:T(8,128)(2,1)S(1)}, bf16[128,512]{1,0:T(8,128)(2,1)}, u32[]{:S(2)}) copy-start(bf16[128,512]{1,0:T(8,128)(2,1)} %param.22) | copy-start | bytes 393220
  94.9 1.8 %copy-start.9 = (bf16[128,128]{1,0:T(8,128)(2,1)S(1)}, bf16[128,128]{1,0:T(8,128)(2,1)}, u32[]{:S(2)}) copy-start(bf16[128,128]{1,0:T(8,128)(2,1)} %param.21) | copy-start | bytes 98308
  94.9 1.8 %copy-start.11 = (bf16[10,160,4]{1,2,0:T(4,128)(2,1)S(1)}, bf16[10,160,4]{1,2,0:T(4,128)(2,1)}, u32[]{:S(2)}) copy-start(bf16[10,160,4]{1,2,0:T(4,128)(2,1)} %custom-call) | copy-start | bytes 38404
  94.9 1.8 %copy-start.16 = (bf16[128,4]{0,1:T(4,128)(2,1)S(1)}, bf16[128,4]{0,1:T(4,128)(2,1)}, u32[]{:S(2)}) copy-start(bf16[128,4]{0,1:T(4,128)(2,1)} %convert.12) | copy-start | bytes 3076
  96.7 43.3 %copy-start.12 = (f32[160]{0:T(256)S(1)}, f32[160]{0:T(256)}, u32[]{:S(2)}) copy-start(f32[160]{0:T(256)} %add_multiply_fusion) | copy-start | bytes 1924
  96.7 43.3 %copy-start.17 = (f32[4]{0:T(128)S(1)}, f32[4]{0:T(128)}, u32[]{:S(2)}) copy-start(f32[4]{0:T(128)} %param.24) | copy-start | bytes 52
  117.8 0.8 copy-start.8
  117.8 0.9 copy-start.4
  141.1 1.1 copy-start.10
  142.2 28.4 %copy-start.5 = (bf16[10,160,128]{2,1,0:T(8,128)(2,1)S(1)}, bf16[10,160,128]{2,1,0:T(8,128)(2,1)}, u32[]{:S(2)}) copy-start(bf16[10,160,128]{2,1,0:T(8,128)(2,1)} %copy-done.4) | copy-start | bytes 1228804
where the time goes:
time: 174 us; the launch traced here: 172 us
  blocking collectives  44.1 us (25%)
  local copies, waits for them, and re-layouts  34.8 us (20%)
  waiting for transfers between devices  30.9 us (18%)
  other arithmetic  29.4 us (17%)
  matrix products  19.3 us (11%)
  starting transfers between devices  11.2 us (6%)
    dynamic_slice x60, local copies, waits for them, and re-layouts, per_device(): left_proj, right_proj, out_gate = lax.map(project_row, (pair, row_mask))  25.1 us
    all_to_all x1, blocking collectives, per_device(): lax.all_to_all(right_lay, 'row', split_axis=0, concat_axis=2, tiled=True)  22.8 us
    all_gather x1, blocking collectives, per_device(): full_bias = lax.all_gather(bias_lay, 'row', axis=1, tiled=True)  21.3 us
    all_to_all x1, waiting for transfers between devices, per_device(): lax.all_to_all(left_lay, 'row', split_axis=0, concat_axis=2, tiled=True)  16.3 us
    all_to_all x1, waiting for transfers between devices, per_device(): lax.all_to_all(product.astype(jnp.bfloat16)[None], 'row', split_axis=2, c...  14.6 us
    dynamic_update_slice x40, other arithmetic, per_device(): left_proj, right_proj, out_gate = lax.map(project_row, (pair, row_mask))  8.31 us
    all_to_all x1, starting transfers between devices, per_device(): lax.all_to_all(left_lay, 'row', split_axis=0, concat_axis=2, tiled=True)  7.52 us
    mul x10, other arithmetic, project_row(): weight = (mask_value * mask_float)[:, None]  6.19 us
  transfers between devices with their start and end apart: 2, of which 2 were waited for; matrix products, arithmetic and copies ran while one was open for 1% of the time, Pallas kernels for 0%

commit v1 on v0

--- a/solution.py
+++ b/solution.py
@@ -1,7 +1,14 @@
 import jax
 import jax.numpy as jnp
 from jax import lax
+from jax.experimental import pallas as pl
+from jax.experimental.pallas import tpu as pltpu
 from jax.sharding import PartitionSpec as P
+
+F32 = jnp.float32
+BF16 = jnp.bfloat16
+NT = (((1,), (1,)), ((), ()))
+TN = (((0,), (0,)), ((), ()))
 
 
 def layer_norm(values):
@@ -42,7 +49,7 @@
     return lax.map(one_row, (query, key, value, att_gate))
 
 
-def per_device(
+def per_device_general(
     pair, mask, chain, tri_proj, tri_gate, tri_out, att_proj, att_bias, same_chain, att_out
 ):
     local_rows, tokens, width = pair.shape
@@ -117,6 +124,375 @@
     )
 
 
+ROWS, TOKENS, WIDTH, PARTS, HEADS = 10, 160, 128, 16, 4
+SHARE = WIDTH // PARTS
+TAIL = TOKENS - 128
+
+
+def dot(left, right, dims):
+    return lax.dot_general(left, right, dims, preferred_element_type=F32)
+
+
+def norm(values, axis):
+    centred = values - jnp.mean(values, axis=axis, keepdims=True)
+    spread = jnp.mean(centred * centred, axis=axis, keepdims=True)
+    return (centred * lax.rsqrt(spread + 1e-05)).astype(BF16)
+
+
+def pad_lanes(values):
+    return jnp.concatenate(
+        [values, jnp.zeros((values.shape[0], 128 - values.shape[1]), values.dtype)], axis=1
+    )
+
+
+def fused_kernel(
+    mask_s,
+    same_s,
+    pair,
+    mask_v,
+    chain_v,
+    tri_proj,
+    tri_gate,
+    tri_out,
+    att_proj,
+    bias_t,
+    att_out,
+    out,
+    proj_t,
+    normed,
+    tails,
+    send1,
+    recv1,
+    main_f,
+    tail_f,
+    sum_m,
+    sum_t,
+    send2,
+    recv2,
+    recv2_f,
+    summed,
+    gate,
+    mid,
+    mid_norm,
+    bias_rows,
+    send3,
+    recv3,
+    bias_m,
+    bias_tl,
+    logit,
+    query,
+    key,
+    value,
+    att_gate,
+    sends,
+    recvs,
+):
+    me = lax.axis_index("row")
+
+    def other(step):
+        return lax.rem(me + step, PARTS)
+
+    barrier = pltpu.get_barrier_semaphore()
+
+    @pl.loop(1, PARTS)
+    def _(step):
+        pl.semaphore_signal(
+            barrier, inc=1, device_id={"row": other(step)}, device_id_type=pl.DeviceIdType.MESH
+        )
+
+    def copy_to(phase, source, landing, part):
+        return pltpu.make_async_remote_copy(
+            src_ref=source,
+            dst_ref=landing.at[me],
+            send_sem=sends.at[phase, part],
+            recv_sem=recvs.at[phase, me],
+            device_id={"row": part},
+            device_id_type=pl.DeviceIdType.MESH,
+        )
+
+    def arrived(phase, landing, source):
+        return pltpu.make_async_remote_copy(
+            src_ref=landing.at[source],
+            dst_ref=landing.at[source],
+            send_sem=sends.at[phase, source],
+            recv_sem=recvs.at[phase, source],
+            device_id={"row": source},
+            device_id_type=pl.DeviceIdType.MESH,
+        )
+
+    turned = tri_proj[...].astype(F32).T
+    pieces = []
+    for half in range(2):
+        for part in range(PARTS):
+            for side in range(2):
+                at = half * 2 * WIDTH + side * WIDTH + part * SHARE
+                pieces.append(turned[at : at + SHARE])
+    proj_t[...] = jnp.concatenate(pieces, axis=0).astype(BF16)
+    mask_row = mask_v[...].astype(F32)
+
+    @pl.loop(0, ROWS)
+    def _(i):
+        row = norm(pair[i].astype(F32), 1)
+        normed[i] = row
+        projected = dot(proj_t[...], row, NT)
+        weight = mask_row * mask_s[me * ROWS + i].astype(F32)
+        both = weight * jax.nn.sigmoid(projected[2 * WIDTH :]) * projected[: 2 * WIDTH]
+        send1[:, i] = both[:, :128].astype(BF16).reshape(PARTS, 16, 128)
+        tails[i] = both[:, 128:]
+
+    for tile in range(3):
+        parts = [tails[i] for i in range(4 * tile, min(4 * tile + 4, ROWS))]
+        packed = jnp.concatenate(parts, axis=1)
+        if len(parts) < 4:
+            packed = pad_lanes(packed)
+        send1[:, ROWS + tile] = packed.astype(BF16).reshape(PARTS, 16, 128)
+
+    pl.semaphore_wait(barrier, PARTS - 1)
+
+    @pl.loop(1, PARTS)
+    def _(step):
+        part = other(step)
+        copy_to(0, send1.at[part], recv1, part).start()
+
+    recv1[me] = send1[me]
+
+    @pl.loop(0, ROWS)
+    def _(i):
+        gate[i] = jax.nn.sigmoid(jnp.dot(normed[i], tri_gate[...], preferred_element_type=F32))
+
+    @pl.loop(0, PARTS)
+    def _(step):
+        source = other(step)
+
+        @pl.when(step > 0)
+        def _():
+            arrived(0, recv1, source).wait_recv()
+
+        for i in range(ROWS):
+            at = pl.multiple_of((source * ROWS + i) * 16, 16)
+            main_f[pl.ds(at, 16), :] = recv1[source, i].astype(F32)
+            lane = TAIL * (i % 4)
+            tail = recv1[source, ROWS + i // 4].astype(F32)[:, lane : lane + TAIL]
+            tail_f[pl.ds(at, 16), 0:TAIL] = tail
+
+    for c in range(SHARE):
+        at_l, at_r = pl.ds(c, TOKENS, stride=16), pl.ds(SHARE + c, TOKENS, stride=16)
+        main = dot(main_f[at_l, :].astype(BF16), main_f[at_r, :].astype(BF16), NT)
+        tail = dot(
+            tail_f[at_l, :][:, :TAIL].astype(BF16), tail_f[at_r, :][:, :TAIL].astype(BF16), NT
+        )
+        total = main + tail
+        sum_m[pl.ds(c, TOKENS, stride=SHARE), :] = total[:, :128]
+        sum_t[pl.ds(c, TOKENS, stride=SHARE), :] = pad_lanes(total[:, 128:])
+
+    @pl.loop(0, PARTS)
+    def _(step):
+        part = other(step)
+        at = pl.multiple_of(part * ROWS * SHARE, ROWS * SHARE)
+        send2[part, 0:80] = sum_m[pl.ds(at, 80), :].astype(BF16)
+        rest = sum_t[pl.ds(at, 80), :][:, :TAIL]
+        packed = jnp.concatenate([rest[16 * t : 16 * t + 16] for t in range(4)], axis=1)
+        send2[part, 80:96] = packed.astype(BF16)
+        send2[part, 96:112] = pad_lanes(rest[64:80]).astype(BF16)
+
+        @pl.when(step > 0)
+        def _():
+            copy_to(1, send2.at[part], recv2, part).start()
+
+    recv2[me] = send2[me]
+
+    @pl.loop(0, PARTS)
+    def _(step):
+        source = other(step)
+
+        @pl.when(step > 0)
+        def _():
+            arrived(1, recv2, source).wait_recv()
+
+        recv2_f[source] = recv2[source].astype(F32)
+
+    for i in range(ROWS):
+        summed[i, :, 0:128] = recv2_f[:, SHARE * i : SHARE * i + SHARE, :].reshape(WIDTH, 128)
+        row = 80 + SHARE * (i % 2) + (16 if i >= 8 else 0)
+        lane = TAIL * ((i // 2) % 4)
+        rest = recv2_f[:, row : row + SHARE, :].reshape(WIDTH, 128)
+        summed[i, :, 128:TOKENS] = rest[:, lane : lane + TAIL]
+
+    @pl.loop(0, ROWS // 2)
+    def _(pair_at):
+        biases = []
+        for half in range(2):
+            i = pair_at * 2 + half
+            tri_norm = norm(summed[i], 0)
+            update = dot(tri_norm, tri_out[...], TN)
+            mid_row = (pair[i].astype(F32) + gate[i] * update).astype(BF16)
+            mid[i] = mid_row
+            mid_n = norm(mid_row.astype(F32), 1)
+            mid_norm[i] = mid_n
+            bias = dot(bias_t[...], mid_n, NT)
+            biases.append(bias[0:8] + bias[8:16])
+        joined = jnp.concatenate([biases[0][0:HEADS], biases[1][0:HEADS]], axis=0)
+        bias_rows[pl.ds(pl.multiple_of(pair_at * 8, 8), 8), :] = joined
+
+    send3[0:32] = bias_rows[0:32, 0:128].astype(BF16)
+    send3[32:48] = jnp.concatenate(
+        [bias_rows[32:40, 0:128], jnp.zeros((8, 128), F32)], axis=0
+    ).astype(BF16)
+    last = jnp.concatenate([bias_rows[32:40, 128:TOKENS], jnp.zeros((8, TAIL), F32)], axis=0)
+    send3[48:64] = pad_lanes(
+        jnp.concatenate(
+            [bias_rows[0:16, 128:TOKENS], bias_rows[16:32, 128:TOKENS], last], axis=1
+        )
+    ).astype(BF16)
+
+    @pl.loop(1, PARTS)
+    def _(step):
+        part = other(step)
+        copy_to(2, send3, recv3, part).start()
+
+    recv3[me] = send3[...]
+
+    query_t = att_proj[:, 0:WIDTH].astype(F32).T.astype(BF16)
+    channel = lax.broadcasted_iota(jnp.int32, (WIDTH, HEADS * TOKENS), 0) // (WIDTH // HEADS)
+    lane = lax.broadcasted_iota(jnp.int32, (WIDTH, HEADS * TOKENS), 1)
+    block = (lane >= channel * TOKENS) & (lane < channel * TOKENS + TOKENS)
+    scale = (WIDTH // HEADS) ** (-0.5)
+
+    @pl.loop(0, ROWS)
+    def _(i):
+        mid_n = mid_norm[i]
+        rest = jnp.dot(mid_n, att_proj[:, WIDTH:], preferred_element_type=F32)
+        key[i] = rest[:, 0:WIDTH].astype(BF16)
+        value[i] = rest[:, WIDTH : 2 * WIDTH].astype(BF16)
+        att_gate[i] = jax.nn.sigmoid(rest[:, 2 * WIDTH :])
+        wide = dot(query_t, jnp.concatenate([mid_n] * HEADS, axis=0), NT)
+        query[i] = jnp.where(block, wide * scale, 0.0).astype(BF16)
+
+    ids = lax.broadcasted_iota(jnp.int32, (16, TOKENS), 0)
+    one_hot = jnp.where(ids == chain_v[...], 1.0, 0.0).astype(BF16)
+    same = dot(one_hot, one_hot, TN)
+    absent = 10000.0 * (mask_row - 1.0)
+
+    @pl.loop(0, PARTS)
+    def _(step):
+        source = other(step)
+
+        @pl.when(step > 0)
+        def _():
+            arrived(2, recv3, source).wait_recv()
+
+        at = pl.multiple_of(source * 40, 8)
+        got = recv3[source].astype(F32)
+        bias_m[pl.ds(at, 40), :] = got[0:40]
+        for t in range(3):
+            size = 16 if t < 2 else 8
+            bias_tl[pl.ds(pl.multiple_of(at + 16 * t, 8), size), 0:TAIL] = got[
+                48 : 48 + size, TAIL * t : TAIL * t + TAIL
+            ]
+
+    mains, rests = [], []
+    for h in range(HEADS):
+        extra = same_s[h] * same
+        every = pl.ds(h, TOKENS, stride=HEADS)
+        mains.append(bias_m[every, :] + extra[:, 0:128] + absent[:, 0:128])
+        rest = bias_tl[every, :][:, :TAIL] + extra[:, 128:] + absent[:, 128:]
+        rests.append(pad_lanes(rest))
+    logit[0:128, :] = jnp.concatenate(mains, axis=0).T
+    logit[128:TOKENS, :] = jnp.concatenate(rests, axis=0).T[0:TAIL]
+
+    head_of = lax.broadcasted_iota(jnp.int32, (TOKENS, WIDTH), 1) // (WIDTH // HEADS)
+
+    @pl.loop(0, ROWS)
+    def _(i):
+        scores = jnp.dot(key[i], query[i], preferred_element_type=F32) + logit[...]
+        top = jnp.max(scores, axis=0, keepdims=True)
+        exps = jnp.exp(scores - top)
+        weight = (exps * (1.0 / jnp.sum(exps, axis=0, keepdims=True))).astype(BF16)
+        mixes = dot(weight, value[i], TN)
+        mixed = mixes[0:TOKENS]
+        for h in range(1, HEADS):
+            mixed = jnp.where(head_of == h, mixes[h * TOKENS : (h + 1) * TOKENS], mixed)
+        gated = (att_gate[i] * mixed).astype(BF16)
+        added = jnp.dot(gated, att_out[...], preferred_element_type=F32)
+        out[i] = (mid[i].astype(F32) + added).astype(BF16)
+
+    @pl.loop(1, PARTS)
+    def _(step):
+        part = other(step)
+        copy_to(0, send1.at[part], recv1, part).wait_send()
+        copy_to(1, send2.at[part], recv2, part).wait_send()
+        copy_to(2, send3, recv3, part).wait_send()
+
+
+def per_device_fused(
+    pair, mask, chain, tri_proj, tri_gate, tri_out, att_proj, att_bias, same_chain, att_out
+):
+    turned = att_bias.T
+    high = turned.astype(BF16)
+    low = (turned - high.astype(F32)).astype(BF16)
+    zeros = jnp.zeros((HEADS, WIDTH), BF16)
+    bias_t = jnp.concatenate([high, zeros, low, zeros], axis=0)
+    smem = pl.BlockSpec(memory_space=pltpu.SMEM)
+    vmem = pl.BlockSpec(memory_space=pltpu.VMEM)
+    all_rows = (ROWS, TOKENS, WIDTH)
+    return pl.pallas_call(
+        fused_kernel,
+        out_shape=jax.ShapeDtypeStruct(all_rows, BF16),
+        in_specs=[smem, smem] + [vmem] * 9,
+        out_specs=vmem,
+        scratch_shapes=[
+            pltpu.VMEM((4 * WIDTH, WIDTH), BF16),
+            pltpu.VMEM(all_rows, BF16),
+            pltpu.VMEM((ROWS, 2 * WIDTH, TAIL), F32),
+            pltpu.VMEM((PARTS, 13, 16, 128), BF16),
+            pltpu.VMEM((PARTS, 13, 16, 128), BF16),
+            pltpu.VMEM((TOKENS * 16, 128), F32),
+            pltpu.VMEM((TOKENS * 16, 128), F32),
+            pltpu.VMEM((TOKENS * SHARE, 128), F32),
+            pltpu.VMEM((TOKENS * SHARE, 128), F32),
+            pltpu.VMEM((PARTS, 112, 128), BF16),
+            pltpu.VMEM((PARTS, 112, 128), BF16),
+            pltpu.VMEM((PARTS, 112, 128), F32),
+            pltpu.VMEM((ROWS, WIDTH, TOKENS), F32),
+            pltpu.VMEM(all_rows, F32),
+            pltpu.VMEM(all_rows, BF16),
+            pltpu.VMEM(all_rows, BF16),
+            pltpu.VMEM((40, TOKENS), F32),
+            pltpu.VMEM((64, 128), BF16),
+            pltpu.VMEM((PARTS, 64, 128), BF16),
+            pltpu.VMEM((TOKENS * HEADS, 128), F32),
+            pltpu.VMEM((TOKENS * HEADS, 128), F32),
+            pltpu.VMEM((TOKENS, HEADS * TOKENS), F32),
+            pltpu.VMEM((ROWS, WIDTH, HEADS * TOKENS), BF16),
+            pltpu.VMEM(all_rows, BF16),
+            pltpu.VMEM(all_rows, BF16),
+            pltpu.VMEM(all_rows, F32),
+            pltpu.SemaphoreType.DMA((3, PARTS)),
+            pltpu.SemaphoreType.DMA((3, PARTS)),
+        ],
+        compiler_params=pltpu.CompilerParams(
+            collective_id=0, has_side_effects=True, vmem_limit_bytes=40 * 1024 * 1024
+        ),
+    )(
+        mask,
+        same_chain,
+        pair,
+        mask.reshape(1, TOKENS),
+        chain.reshape(1, TOKENS),
+        tri_proj,
+        tri_gate,
+        tri_out,
+        att_proj,
+        bias_t,
+        att_out,
+    )
+
+
+def per_device(pair, *others):
+    fits = pair.shape == (ROWS, TOKENS, WIDTH) and lax.axis_size("row") == PARTS
+    return (per_device_fused if fits else per_device_general)(pair, *others)
+
+
 def solution(mesh):
     return jax.shard_map(
         per_device,

time: 174 us -> 65 us (0.37)
  Pallas kernels: 0 us -> 57.1 us
  blocking collectives: 44.1 us -> 0 us
  waiting for transfers between devices: 30.9 us -> 0 us
  other arithmetic: 29.4 us -> 0.02 us
  local copies, waits for them, and re-layouts: 34.8 us -> 7.18 us
  matrix products: 19.3 us -> 0 us
  starting transfers between devices: 11.2 us -> 0 us
    pallas_call x0 -> x1, Pallas kernels: none -> 57.1 us  [per_device_fused(): pl.pallas_call(fused_kernel, out_shape=jax.ShapeDtypeStruct(all_rows, BF1...]
    all_to_all x2 -> x0, waiting for transfers between devices: 30.9 us -> none  [the longest x1 16.3 us: per_device(): lax.all_to_all(left_lay, 'row', split_axis=0, concat_axis=2, tiled=True)]
    dynamic_slice x81 -> x0, local copies, waits for them, and re-layouts: 26.2 us -> none  [the longest x60 25.1 us: per_device(): left_proj, right_proj, out_gate = lax.map(project_row, (pair, row_mask))]
    all_to_all x1 -> x0, blocking collectives: 22.8 us -> none  [per_device(): lax.all_to_all(right_lay, 'row', split_axis=0, concat_axis=2, tiled=True)]
    all_gather x1 -> x0, blocking collectives: 21.3 us -> none  [per_device(): full_bias = lax.all_gather(bias_lay, 'row', axis=1, tiled=True)]
    dot_general x72 -> x0, matrix products: 19.3 us -> none  [the longest x10 2.93 us: one_row(): jnp.einsum('jhd,khd->hjk', query_heads, key_heads, preferred_element_type...]
    all_to_all x2 -> x0, starting transfers between devices: 11.2 us -> none  [the longest x1 7.52 us: per_device(): lax.all_to_all(left_lay, 'row', split_axis=0, concat_axis=2, tiled=True)]
    reduce_sum x60 -> x0, other arithmetic: 9.18 us -> none  [the longest x30 5.68 us: layer_norm(): spread = jnp.mean(centred * centred, axis=-1, keepdims=True)]
  transfers between devices with their start and end apart: 2 -> 0, of which waited for: 2 -> 0; matrix products, arithmetic and copies ran while one was open for 1% -> 0% of each run, Pallas kernels for 0% -> 0%
where the time goes in v1:
time: 65 us; the launch traced here: 64.3 us
  Pallas kernels  57.1 us (88%)
  local copies, waits for them, and re-layouts  7.18 us (11%)
    pallas_call x1, Pallas kernels, per_device_fused(): pl.pallas_call(fused_kernel, out_shape=jax.ShapeDtypeStruct(all_rows, BF1...  57.1 us
    unnamed x21, local copies, waits for them, and re-layouts  7.18 us

profile of v1, /device:TPU:0, one launch (start us, length us, event | category | flops | bytes accessed | tf_op | source)
XLA Modules:
  0.0 64.3 jit_solution(4291425954174475170)
XLA Ops:
  0.0 0.0 copy-start.9
  0.0 0.7 %copy-done.9 = f32[128,4]{0,1:T(4,128)S(1)} copy-done((f32[128,4]{0,1:T(4,128)S(1)}, f32[128,4]{0,1:T(4,128)}, u32[]{:S(2)}) %copy-start.9) | copy-done | bytes 2072
  0.7 0.0 copy-start.6
  0.7 0.0 copy-start.7
  0.7 0.0 copy-start.8
  0.7 0.6 copy-done.6
  1.4 0.0 copy-done.7
  1.4 0.0 copy-done.8
  1.4 0.0 copy-start
  1.4 1.0 %copy-done = bf16[10,160,128]{2,1,0:T(8,128)(2,1)S(1)} copy-done((bf16[10,160,128]{2,1,0:T(8,128)(2,1)S(1)}, bf16[10,160,128]{2,1,0:T(8,128)(2,1)}, u32[]{:S(2)}) %copy-start) | copy-done | bytes 409624
  2.4 0.0 copy-start.1
  2.4 0.9 %copy-done.1 = bf16[128,512]{1,0:T(8,128)(2,1)S(1)} copy-done((bf16[128,512]{1,0:T(8,128)(2,1)S(1)}, bf16[128,512]{1,0:T(8,128)(2,1)}, u32[]{:S(2)}) %copy-start.1) | copy-done | bytes 131096
  3.3 0.0 copy-start.2
  3.3 0.9 %copy-done.2 = bf16[128,512]{1,0:T(8,128)(2,1)S(1)} copy-done((bf16[128,512]{1,0:T(8,128)(2,1)S(1)}, bf16[128,512]{1,0:T(8,128)(2,1)}, u32[]{:S(2)}) %copy-start.2) | copy-done | bytes 131096
  4.2 0.0 copy-start.3
  4.2 0.8 %copy-done.3 = bf16[128,128]{1,0:T(8,128)(2,1)S(1)} copy-done((bf16[128,128]{1,0:T(8,128)(2,1)S(1)}, bf16[128,128]{1,0:T(8,128)(2,1)}, u32[]{:S(2)}) %copy-start.3) | copy-done | bytes 32792
  5.0 0.0 copy-start.4
  5.0 0.8 %copy-done.4 = bf16[128,128]{1,0:T(8,128)(2,1)S(1)} copy-done((bf16[128,128]{1,0:T(8,128)(2,1)S(1)}, bf16[128,128]{1,0:T(8,128)(2,1)}, u32[]{:S(2)}) %copy-start.4) | copy-done | bytes 32792
  5.7 0.0 copy-start.5
  5.7 0.8 %copy-done.5 = bf16[128,128]{1,0:T(8,128)(2,1)S(1)} copy-done((bf16[128,128]{1,0:T(8,128)(2,1)S(1)}, bf16[128,128]{1,0:T(8,128)(2,1)}, u32[]{:S(2)}) %copy-start.5) | copy-done | bytes 32792
  6.5 57.1 %shard_map.100 = bf16[10,160,128]{2,1,0:T(8,128)(2,1)S(1)} custom-call(s32[160]{0:T(256)S(1)} %copy-done.6, f32[4]{0:T(128)S(1)} %copy-done.8, bf16[10,160,128]{2,1,0:T(8,128)(2,1)S(1)} %copy-done, s32[1,160]{1,0:T(1,128)S(1)} %bitcast.8, s32[1,160]{1,0:T(1,128)S(1)} %bitcast.9, bf16[128,512]{1,0:T(8,128)(2,1)S(1)} %copy-done.1, ...), custom_call_target="tpu_custom_call" | custom-call | tf_op jit(solution)/shard_map/pallas_call | solution.py:438
  63.6 0.8 %copy.12 = bf16[10,160,128]{2,1,0:T(8,128)(2,1)} copy(bf16[10,160,128]{2,1,0:T(8,128)(2,1)S(1)} %shard_map.100) | data formatting | bytes 819200
  (3 shorter events, 0.0 us)
Async XLA Ops:
  0.0 0.7 %copy-start.9 = (f32[128,4]{0,1:T(4,128)S(1)}, f32[128,4]{0,1:T(4,128)}, u32[]{:S(2)}) copy-start(f32[128,4]{0,1:T(4,128)} %param.17) | copy-start | bytes 6148
  0.7 0.7 %copy-start.6 = (s32[160]{0:T(256)S(1)}, s32[160]{0:T(256)}, u32[]{:S(2)}) copy-start(s32[160]{0:T(256)} %mask_s.1) | copy-start | bytes 1924
  0.7 0.7 %copy-start.7 = (s32[160]{0:T(256)S(1)}, s32[160]{0:T(256)}, u32[]{:S(2)}) copy-start(s32[160]{0:T(256)} %param.12) | copy-start | bytes 1924
  0.7 0.7 %copy-start.8 = (f32[4]{0:T(128)S(1)}, f32[4]{0:T(128)}, u32[]{:S(2)}) copy-start(f32[4]{0:T(128)} %same_s.1) | copy-start | bytes 52
  1.4 1.0 %copy-start = (bf16[10,160,128]{2,1,0:T(8,128)(2,1)S(1)}, bf16[10,160,128]{2,1,0:T(8,128)(2,1)}, u32[]{:S(2)}) copy-start(bf16[10,160,128]{2,1,0:T(8,128)(2,1)} %pair.1) | copy-start | bytes 1228804
  2.4 0.9 %copy-start.1 = (bf16[128,512]{1,0:T(8,128)(2,1)S(1)}, bf16[128,512]{1,0:T(8,128)(2,1)}, u32[]{:S(2)}) copy-start(bf16[128,512]{1,0:T(8,128)(2,1)} %tri_proj.1) | copy-start | bytes 393220
  3.3 0.9 %copy-start.2 = (bf16[128,512]{1,0:T(8,128)(2,1)S(1)}, bf16[128,512]{1,0:T(8,128)(2,1)}, u32[]{:S(2)}) copy-start(bf16[128,512]{1,0:T(8,128)(2,1)} %att_proj.1) | copy-start | bytes 393220
  4.2 0.8 %copy-start.3 = (bf16[128,128]{1,0:T(8,128)(2,1)S(1)}, bf16[128,128]{1,0:T(8,128)(2,1)}, u32[]{:S(2)}) copy-start(bf16[128,128]{1,0:T(8,128)(2,1)} %tri_gate.1) | copy-start | bytes 98308
  5.0 0.8 %copy-start.4 = (bf16[128,128]{1,0:T(8,128)(2,1)S(1)}, bf16[128,128]{1,0:T(8,128)(2,1)}, u32[]{:S(2)}) copy-start(bf16[128,128]{1,0:T(8,128)(2,1)} %tri_out.1) | copy-start | bytes 98308
  5.7 0.8 %copy-start.5 = (bf16[128,128]{1,0:T(8,128)(2,1)S(1)}, bf16[128,128]{1,0:T(8,128)(2,1)}, u32[]{:S(2)}) copy-start(bf16[128,128]{1,0:T(8,128)(2,1)} %att_out.1) | copy-start | bytes 98308

commit v2 on v1

--- a/solution.py
+++ b/solution.py
@@ -146,18 +146,32 @@
 
 
 def fused_kernel(
-    mask_s,
-    same_s,
+    *refs,
+):
+    outside, (out, *inside, loads) = refs[:10], refs[10:]
+    held, scratch = inside[:10], inside[10:]
+    fetches = [
+        pltpu.make_async_copy(source, target, loads.at[k])
+        for k, (source, target) in enumerate(zip(outside, held))
+    ]
+    for fetch in fetches:
+        fetch.start()
+    fused_body(fetches, out, *held, *scratch)
+
+
+def fused_body(
+    fetches,
+    out,
     pair,
+    tri_proj,
     mask_v,
-    chain_v,
-    tri_proj,
     tri_gate,
     tri_out,
+    bias_t,
     att_proj,
-    bias_t,
+    chain_v,
+    same_v,
     att_out,
-    out,
     proj_t,
     normed,
     tails,
@@ -220,6 +234,9 @@
             device_id_type=pl.DeviceIdType.MESH,
         )
 
+    for fetch in fetches[:3]:
+        fetch.wait()
+
     turned = tri_proj[...].astype(F32).T
     pieces = []
     for half in range(2):
@@ -229,13 +246,15 @@
                 pieces.append(turned[at : at + SHARE])
     proj_t[...] = jnp.concatenate(pieces, axis=0).astype(BF16)
     mask_row = mask_v[...].astype(F32)
+    token = lax.broadcasted_iota(jnp.int32, (1, TOKENS), 1)
 
     @pl.loop(0, ROWS)
     def _(i):
         row = norm(pair[i].astype(F32), 1)
         normed[i] = row
         projected = dot(proj_t[...], row, NT)
-        weight = mask_row * mask_s[me * ROWS + i].astype(F32)
+        mine = jnp.where(token == me * ROWS + i, mask_row, 0.0)
+        weight = mask_row * jnp.sum(mine, axis=1, keepdims=True)
         both = weight * jax.nn.sigmoid(projected[2 * WIDTH :]) * projected[: 2 * WIDTH]
         send1[:, i] = both[:, :128].astype(BF16).reshape(PARTS, 16, 128)
         tails[i] = both[:, 128:]
@@ -255,6 +274,8 @@
         copy_to(0, send1.at[part], recv1, part).start()
 
     recv1[me] = send1[me]
+    for fetch in fetches[3:]:
+        fetch.wait()
 
     @pl.loop(0, ROWS)
     def _(i):
@@ -392,7 +413,7 @@
 
     mains, rests = [], []
     for h in range(HEADS):
-        extra = same_s[h] * same
+        extra = same_v[0:1, h : h + 1] * same
         every = pl.ds(h, TOKENS, stride=HEADS)
         mains.append(bias_m[every, :] + extra[:, 0:128] + absent[:, 0:128])
         rest = bias_tl[every, :][:, :TAIL] + extra[:, 128:] + absent[:, 128:]
@@ -432,15 +453,28 @@
     low = (turned - high.astype(F32)).astype(BF16)
     zeros = jnp.zeros((HEADS, WIDTH), BF16)
     bias_t = jnp.concatenate([high, zeros, low, zeros], axis=0)
-    smem = pl.BlockSpec(memory_space=pltpu.SMEM)
+    hbm = pl.BlockSpec(memory_space=pltpu.HBM)
     vmem = pl.BlockSpec(memory_space=pltpu.VMEM)
     all_rows = (ROWS, TOKENS, WIDTH)
+    inputs = (
+        pair,
+        tri_proj,
+        mask.reshape(1, TOKENS),
+        tri_gate,
+        tri_out,
+        bias_t,
+        att_proj,
+        chain.reshape(1, TOKENS),
+        same_chain.reshape(1, HEADS),
+        att_out,
+    )
     return pl.pallas_call(
         fused_kernel,
         out_shape=jax.ShapeDtypeStruct(all_rows, BF16),
-        in_specs=[smem, smem] + [vmem] * 9,
+        in_specs=[hbm] * 10,
         out_specs=vmem,
-        scratch_shapes=[
+        scratch_shapes=[pltpu.VMEM(each.shape, each.dtype) for each in inputs]
+        + [
             pltpu.VMEM((4 * WIDTH, WIDTH), BF16),
             pltpu.VMEM(all_rows, BF16),
             pltpu.VMEM((ROWS, 2 * WIDTH, TAIL), F32),
@@ -469,23 +503,12 @@
             pltpu.VMEM(all_rows, F32),
             pltpu.SemaphoreType.DMA((3, PARTS)),
             pltpu.SemaphoreType.DMA((3, PARTS)),
+            pltpu.SemaphoreType.DMA((10,)),
         ],
         compiler_params=pltpu.CompilerParams(
             collective_id=0, has_side_effects=True, vmem_limit_bytes=40 * 1024 * 1024
         ),
-    )(
-        mask,
-        same_chain,
-        pair,
-        mask.reshape(1, TOKENS),
-        chain.reshape(1, TOKENS),
-        tri_proj,
-        tri_gate,
-        tri_out,
-        att_proj,
-        bias_t,
-        att_out,
-    )
+    )(*inputs)
 
 
 def per_device(pair, *others):

time: 65 us -> 65.3 us (level)
  no operation moved by 1% of the time
where the time goes in v2:
time: 65.3 us; the launch traced here: 64.5 us
  Pallas kernels  57.3 us (88%)
  local copies, waits for them, and re-layouts  7.18 us (11%)
    pallas_call x1, Pallas kernels, per_device_fused(): pl.pallas_call(fused_kernel, out_shape=jax.ShapeDtypeStruct(all_rows, BF1...  57.3 us
    unnamed x21, local copies, waits for them, and re-layouts  7.18 us

profile of v2, /device:TPU:0, one launch (start us, length us, event | category | flops | bytes accessed | tf_op | source)
XLA Modules:
  0.0 64.5 jit_solution(7928444024424348880)
XLA Ops:
  0.0 0.0 copy-start.9
  0.0 0.7 %copy-done.9 = f32[128,4]{0,1:T(4,128)S(1)} copy-done((f32[128,4]{0,1:T(4,128)S(1)}, f32[128,4]{0,1:T(4,128)}, u32[]{:S(2)}) %copy-start.9) | copy-done | bytes 2072
  0.7 0.0 copy-start.6
  0.7 0.0 copy-start.7
  0.7 0.0 copy-start.8
  0.7 0.6 copy-done.6
  1.4 0.0 copy-done.7
  1.4 0.0 copy-done.8
  1.4 0.0 copy-start
  1.4 1.0 %copy-done = bf16[10,160,128]{2,1,0:T(8,128)(2,1)S(1)} copy-done((bf16[10,160,128]{2,1,0:T(8,128)(2,1)S(1)}, bf16[10,160,128]{2,1,0:T(8,128)(2,1)}, u32[]{:S(2)}) %copy-start) | copy-done | bytes 409624
  2.4 0.0 copy-start.1
  2.4 0.9 %copy-done.1 = bf16[128,512]{1,0:T(8,128)(2,1)S(1)} copy-done((bf16[128,512]{1,0:T(8,128)(2,1)S(1)}, bf16[128,512]{1,0:T(8,128)(2,1)}, u32[]{:S(2)}) %copy-start.1) | copy-done | bytes 131096
  3.3 0.0 copy-start.2
  3.3 0.9 %copy-done.2 = bf16[128,512]{1,0:T(8,128)(2,1)S(1)} copy-done((bf16[128,512]{1,0:T(8,128)(2,1)S(1)}, bf16[128,512]{1,0:T(8,128)(2,1)}, u32[]{:S(2)}) %copy-start.2) | copy-done | bytes 131096
  4.2 0.0 copy-start.3
  4.2 0.8 %copy-done.3 = bf16[128,128]{1,0:T(8,128)(2,1)S(1)} copy-done((bf16[128,128]{1,0:T(8,128)(2,1)S(1)}, bf16[128,128]{1,0:T(8,128)(2,1)}, u32[]{:S(2)}) %copy-start.3) | copy-done | bytes 32792
  5.0 0.0 copy-start.4
  5.0 0.8 %copy-done.4 = bf16[128,128]{1,0:T(8,128)(2,1)S(1)} copy-done((bf16[128,128]{1,0:T(8,128)(2,1)S(1)}, bf16[128,128]{1,0:T(8,128)(2,1)}, u32[]{:S(2)}) %copy-start.4) | copy-done | bytes 32792
  5.7 0.0 copy-start.5
  5.7 0.8 %copy-done.5 = bf16[128,128]{1,0:T(8,128)(2,1)S(1)} copy-done((bf16[128,128]{1,0:T(8,128)(2,1)S(1)}, bf16[128,128]{1,0:T(8,128)(2,1)}, u32[]{:S(2)}) %copy-start.5) | copy-done | bytes 32792
  6.5 57.3 %shard_map.100 = bf16[10,160,128]{2,1,0:T(8,128)(2,1)S(1)} custom-call(bf16[10,160,128]{2,1,0:T(8,128)(2,1)S(1)} %copy-done, bf16[128,512]{1,0:T(8,128)(2,1)S(1)} %copy-done.1, s32[1,160]{1,0:T(1,128)S(1)} %bitcast.9, bf16[128,128]{1,0:T(8,128)(2,1)S(1)} %copy-done.3, bf16[128,128]{1,0:T(8,128)(2,1)S(1)} %copy-done.4, ...), custom_call_target="tpu_custom_call" | custom-call | tf_op jit(solution)/shard_map/pallas_call | solution.py:471
  63.8 0.8 %copy.12 = bf16[10,160,128]{2,1,0:T(8,128)(2,1)} copy(bf16[10,160,128]{2,1,0:T(8,128)(2,1)S(1)} %shard_map.100) | data formatting | bytes 819200
  (3 shorter events, 0.0 us)
Async XLA Ops:
  0.0 0.7 %copy-start.9 = (f32[128,4]{0,1:T(4,128)S(1)}, f32[128,4]{0,1:T(4,128)}, u32[]{:S(2)}) copy-start(f32[128,4]{0,1:T(4,128)} %param.17) | copy-start | bytes 6148
  0.7 0.7 %copy-start.6 = (s32[160]{0:T(256)S(1)}, s32[160]{0:T(256)}, u32[]{:S(2)}) copy-start(s32[160]{0:T(256)} %param.11) | copy-start | bytes 1924
  0.7 0.7 %copy-start.7 = (s32[160]{0:T(256)S(1)}, s32[160]{0:T(256)}, u32[]{:S(2)}) copy-start(s32[160]{0:T(256)} %param.12) | copy-start | bytes 1924
  0.7 0.7 %copy-start.8 = (f32[4]{0:T(128)S(1)}, f32[4]{0:T(128)}, u32[]{:S(2)}) copy-start(f32[4]{0:T(128)} %param.18) | copy-start | bytes 52
  1.4 1.0 %copy-start = (bf16[10,160,128]{2,1,0:T(8,128)(2,1)S(1)}, bf16[10,160,128]{2,1,0:T(8,128)(2,1)}, u32[]{:S(2)}) copy-start(bf16[10,160,128]{2,1,0:T(8,128)(2,1)} %refs_0_.1) | copy-start | bytes 1228804
  2.4 0.9 %copy-start.1 = (bf16[128,512]{1,0:T(8,128)(2,1)S(1)}, bf16[128,512]{1,0:T(8,128)(2,1)}, u32[]{:S(2)}) copy-start(bf16[128,512]{1,0:T(8,128)(2,1)} %refs_1_.1) | copy-start | bytes 393220
  3.3 0.9 %copy-start.2 = (bf16[128,512]{1,0:T(8,128)(2,1)S(1)}, bf16[128,512]{1,0:T(8,128)(2,1)}, u32[]{:S(2)}) copy-start(bf16[128,512]{1,0:T(8,128)(2,1)} %refs_6_.1) | copy-start | bytes 393220
  4.2 0.8 %copy-start.3 = (bf16[128,128]{1,0:T(8,128)(2,1)S(1)}, bf16[128,128]{1,0:T(8,128)(2,1)}, u32[]{:S(2)}) copy-start(bf16[128,128]{1,0:T(8,128)(2,1)} %refs_3_.1) | copy-start | bytes 98308
  5.0 0.8 %copy-start.4 = (bf16[128,128]{1,0:T(8,128)(2,1)S(1)}, bf16[128,128]{1,0:T(8,128)(2,1)}, u32[]{:S(2)}) copy-start(bf16[128,128]{1,0:T(8,128)(2,1)} %refs_4_.1) | copy-start | bytes 98308
  5.7 0.8 %copy-start.5 = (bf16[128,128]{1,0:T(8,128)(2,1)S(1)}, bf16[128,128]{1,0:T(8,128)(2,1)}, u32[]{:S(2)}) copy-start(bf16[128,128]{1,0:T(8,128)(2,1)} %refs_9_.1) | copy-start | bytes 98308

commit v3 on v2

--- a/solution.py
+++ b/solution.py
@@ -167,7 +167,7 @@
     mask_v,
     tri_gate,
     tri_out,
-    bias_t,
+    bias_v,
     att_proj,
     chain_v,
     same_v,
@@ -339,6 +339,10 @@
         rest = recv2_f[:, row : row + SHARE, :].reshape(WIDTH, 128)
         summed[i, :, 128:TOKENS] = rest[:, lane : lane + TAIL]
 
+    high = bias_v[...].astype(BF16).astype(F32)
+    none = jnp.zeros((HEADS, WIDTH), F32)
+    bias_t = jnp.concatenate([high, none, bias_v[...] - high, none], axis=0).astype(BF16)
+
     @pl.loop(0, ROWS // 2)
     def _(pair_at):
         biases = []
@@ -350,7 +354,7 @@
             mid[i] = mid_row
             mid_n = norm(mid_row.astype(F32), 1)
             mid_norm[i] = mid_n
-            bias = dot(bias_t[...], mid_n, NT)
+            bias = dot(bias_t, mid_n, NT)
             biases.append(bias[0:8] + bias[8:16])
         joined = jnp.concatenate([biases[0][0:HEADS], biases[1][0:HEADS]], axis=0)
         bias_rows[pl.ds(pl.multiple_of(pair_at * 8, 8), 8), :] = joined
@@ -448,11 +452,6 @@
 def per_device_fused(
     pair, mask, chain, tri_proj, tri_gate, tri_out, att_proj, att_bias, same_chain, att_out
 ):
-    turned = att_bias.T
-    high = turned.astype(BF16)
-    low = (turned - high.astype(F32)).astype(BF16)
-    zeros = jnp.zeros((HEADS, WIDTH), BF16)
-    bias_t = jnp.concatenate([high, zeros, low, zeros], axis=0)
     hbm = pl.BlockSpec(memory_space=pltpu.HBM)
     vmem = pl.BlockSpec(memory_space=pltpu.VMEM)
     all_rows = (ROWS, TOKENS, WIDTH)
@@ -462,7 +461,7 @@
         mask.reshape(1, TOKENS),
         tri_gate,
         tri_out,
-        bias_t,
+        att_bias.T,
         att_proj,
         chain.reshape(1, TOKENS),
         same_chain.reshape(1, HEADS),
@@ -506,7 +505,7 @@
             pltpu.SemaphoreType.DMA((10,)),
         ],
         compiler_params=pltpu.CompilerParams(
-            collective_id=0, has_side_effects=True, vmem_limit_bytes=40 * 1024 * 1024
+            collective_id=0, has_side_effects=True, vmem_limit_bytes=64 * 1024 * 1024
         ),
     )(*inputs)
 

time: 65.3 us -> 60.4 us (0.925)
  local copies, waits for them, and re-layouts: 7.18 us -> 1.78 us
  Pallas kernels: 57.3 us -> 58.1 us
    unnamed x21 -> x1, local copies, waits for them, and re-layouts: 7.18 us -> 1.78 us
    pallas_call x1, Pallas kernels: 57.3 us -> 58.1 us  [per_device_fused(): pl.pallas_call(fused_kernel, out_shape=jax.ShapeDtypeStruct(all_rows, BF1...]
where the time goes in v3:
time: 60.4 us; the launch traced here: 59.9 us
  Pallas kernels  58.1 us (96%)
  local copies, waits for them, and re-layouts  1.78 us (3%)
    pallas_call x1, Pallas kernels, per_device_fused(): pl.pallas_call(fused_kernel, out_shape=jax.ShapeDtypeStruct(all_rows, BF1...  58.1 us
    unnamed x1, local copies, waits for them, and re-layouts  1.78 us

profile of v3, /device:TPU:0, one launch (start us, length us, event | category | flops | bytes accessed | tf_op | source)
XLA Modules:
  0.0 59.9 jit_solution(12640642815402547578)
XLA Ops:
  0.0 58.1 %shard_map.100 = bf16[10,160,128]{2,1,0:T(8,128)(2,1)} custom-call(bf16[10,160,128]{2,1,0:T(8,128)(2,1)} %refs_0_.1, bf16[128,512]{1,0:T(8,128)(2,1)} %refs_1_.1, s32[1,160]{1,0:T(1,128)} %bitcast.5, bf16[128,128]{1,0:T(8,128)(2,1)} %refs_3_.1, bf16[128,128]{1,0:T(8,128)(2,1)} %refs_4_.1, f32[4,128]{1,0:T(4,128)} %bitcast.4, bf16[128,512]{1,0:T(8,128)(2,1)} %refs_6_.1, ...), custom_call_target="tpu_custom_call" | custom-call | tf_op jit(solution)/shard_map/pallas_call | solution.py:470
  58.1 1.8 %copy.12 = bf16[10,160,128]{2,1,0:T(8,128)(2,1)} copy(bf16[10,160,128]{2,1,0:T(8,128)(2,1)} %shard_map.100) | data formatting | bytes 819200

commit v4 on v3

--- a/solution.py
+++ b/solution.py
@@ -125,7 +125,10 @@
 
 
 ROWS, TOKENS, WIDTH, PARTS, HEADS = 10, 160, 128, 16, 4
-SHARE = WIDTH // PARTS
+NEAR = PARTS // 2
+SHARE = WIDTH // NEAR
+TILES = 13
+EARLY = 5
 TAIL = TOKENS - 128
 
 
@@ -175,15 +178,18 @@
     proj_t,
     normed,
     tails,
-    send1,
-    recv1,
-    main_f,
-    tail_f,
+    send_l,
+    recv_l,
+    send_r,
+    recv_r,
+    left_m,
+    left_t,
+    right_m,
+    right_t,
     sum_m,
     sum_t,
     send2,
     recv2,
-    recv2_f,
     summed,
     gate,
     mid,
@@ -203,9 +209,15 @@
 ):
     me = lax.axis_index("row")
 
+    place = lax.rem(me, NEAR)
+    first = me - place
+
     def other(step):
         return lax.rem(me + step, PARTS)
 
+    def near(step):
+        return lax.rem(place + step, NEAR)
+
     barrier = pltpu.get_barrier_semaphore()
 
     @pl.loop(1, PARTS)
@@ -214,37 +226,47 @@
             barrier, inc=1, device_id={"row": other(step)}, device_id_type=pl.DeviceIdType.MESH
         )
 
-    def copy_to(phase, source, landing, part):
+    def copy_to(sent, phase, source, landing, slot, part):
         return pltpu.make_async_remote_copy(
             src_ref=source,
-            dst_ref=landing.at[me],
-            send_sem=sends.at[phase, part],
-            recv_sem=recvs.at[phase, me],
+            dst_ref=landing.at[slot],
+            send_sem=sends.at[sent, part],
+            recv_sem=recvs.at[phase, slot],
             device_id={"row": part},
             device_id_type=pl.DeviceIdType.MESH,
         )
 
-    def arrived(phase, landing, source):
+    def arrived(phase, landing, slot):
         return pltpu.make_async_remote_copy(
-            src_ref=landing.at[source],
-            dst_ref=landing.at[source],
-            send_sem=sends.at[phase, source],
-            recv_sem=recvs.at[phase, source],
-            device_id={"row": source},
+            src_ref=landing.at[slot],
+            dst_ref=landing.at[slot],
+            send_sem=sends.at[phase, slot],
+            recv_sem=recvs.at[phase, slot],
+            device_id={"row": other(1)},
             device_id_type=pl.DeviceIdType.MESH,
         )
+
+    def right_copy(part):
+        return copy_to(0, 0, send_r.at[lax.rem(part, NEAR)], recv_r, me, part)
+
+    def sum_copy(slot):
+        return copy_to(1, 1, send2.at[slot], recv2, place, first + slot)
+
+    def bias_copy(part):
+        return copy_to(2, 2, send3, recv3, me, part)
+
+    def left_copy(slot):
+        return copy_to(3, 3, send_l.at[slot], recv_l, place, first + slot)
+
+    def passed_copy(slot):
+        return copy_to(4, 2, recv3.at[across], recv3, across, first + slot)
+
+    across = lax.rem(me + NEAR, PARTS)
 
     for fetch in fetches[:3]:
         fetch.wait()
 
-    turned = tri_proj[...].astype(F32).T
-    pieces = []
-    for half in range(2):
-        for part in range(PARTS):
-            for side in range(2):
-                at = half * 2 * WIDTH + side * WIDTH + part * SHARE
-                pieces.append(turned[at : at + SHARE])
-    proj_t[...] = jnp.concatenate(pieces, axis=0).astype(BF16)
+    proj_t[...] = tri_proj[...].astype(F32).T.astype(BF16)
     mask_row = mask_v[...].astype(F32)
     token = lax.broadcasted_iota(jnp.int32, (1, TOKENS), 1)
 
@@ -256,7 +278,9 @@
         mine = jnp.where(token == me * ROWS + i, mask_row, 0.0)
         weight = mask_row * jnp.sum(mine, axis=1, keepdims=True)
         both = weight * jax.nn.sigmoid(projected[2 * WIDTH :]) * projected[: 2 * WIDTH]
-        send1[:, i] = both[:, :128].astype(BF16).reshape(PARTS, 16, 128)
+        main = both[:, :128].astype(BF16)
+        send_l[:, i] = main[:WIDTH].reshape(NEAR, SHARE, 128)
+        send_r[:, i] = main[WIDTH:].reshape(NEAR, SHARE, 128)
         tails[i] = both[:, 128:]
 
     for tile in range(3):
@@ -264,16 +288,23 @@
         packed = jnp.concatenate(parts, axis=1)
         if len(parts) < 4:
             packed = pad_lanes(packed)
-        send1[:, ROWS + tile] = packed.astype(BF16).reshape(PARTS, 16, 128)
+        packed = packed.astype(BF16)
+        send_l[:, ROWS + tile] = packed[:WIDTH].reshape(NEAR, SHARE, 128)
+        send_r[:, ROWS + tile] = packed[WIDTH:].reshape(NEAR, SHARE, 128)
 
     pl.semaphore_wait(barrier, PARTS - 1)
 
-    @pl.loop(1, PARTS)
-    def _(step):
-        part = other(step)
-        copy_to(0, send1.at[part], recv1, part).start()
-
-    recv1[me] = send1[me]
+    @pl.loop(0, NEAR)
+    def _(step):
+        right_copy(lax.rem(across - place + near(step), PARTS)).start()
+
+    @pl.loop(1, NEAR)
+    def _(step):
+        right_copy(first + near(step)).start()
+        left_copy(near(step)).start()
+
+    recv_l[place] = send_l[place]
+    recv_r[me] = send_r[place]
     for fetch in fetches[3:]:
         fetch.wait()
 
@@ -281,62 +312,69 @@
     def _(i):
         gate[i] = jax.nn.sigmoid(jnp.dot(normed[i], tri_gate[...], preferred_element_type=F32))
 
-    @pl.loop(0, PARTS)
-    def _(step):
-        source = other(step)
+    def unpack(landing, slot, main_f, tail_f):
+        for i in range(ROWS):
+            at = pl.ds(pl.multiple_of((slot * ROWS + i) * SHARE, SHARE), SHARE)
+            main_f[at, :] = landing[slot, i].astype(F32)
+            lane = TAIL * (i % 4)
+            tail = landing[slot, ROWS + i // 4].astype(F32)[:, lane : lane + TAIL]
+            tail_f[at, 0:TAIL] = tail
+
+    @pl.loop(0, NEAR)
+    def _(step):
+        slot = near(step)
 
         @pl.when(step > 0)
         def _():
-            arrived(0, recv1, source).wait_recv()
-
-        for i in range(ROWS):
-            at = pl.multiple_of((source * ROWS + i) * 16, 16)
-            main_f[pl.ds(at, 16), :] = recv1[source, i].astype(F32)
-            lane = TAIL * (i % 4)
-            tail = recv1[source, ROWS + i // 4].astype(F32)[:, lane : lane + TAIL]
-            tail_f[pl.ds(at, 16), 0:TAIL] = tail
+            arrived(3, recv_l, slot).wait_recv()
+            arrived(0, recv_r, first + slot).wait_recv()
+
+        unpack(recv_l, slot, left_m, left_t)
+        unpack(recv_r, first + slot, right_m, right_t)
+
+    @pl.loop(0, NEAR)
+    def _(step):
+        source = across - place + near(step)
+        arrived(0, recv_r, source).wait_recv()
+        unpack(recv_r, source, right_m, right_t)
 
     for c in range(SHARE):
-        at_l, at_r = pl.ds(c, TOKENS, stride=16), pl.ds(SHARE + c, TOKENS, stride=16)
-        main = dot(main_f[at_l, :].astype(BF16), main_f[at_r, :].astype(BF16), NT)
+        at_l, at_r = pl.ds(c, TOKENS // 2, stride=SHARE), pl.ds(c, TOKENS, stride=SHARE)
+        main = dot(left_m[at_l, :].astype(BF16), right_m[at_r, :].astype(BF16), NT)
         tail = dot(
-            tail_f[at_l, :][:, :TAIL].astype(BF16), tail_f[at_r, :][:, :TAIL].astype(BF16), NT
+            left_t[at_l, :][:, :TAIL].astype(BF16), right_t[at_r, :][:, :TAIL].astype(BF16), NT
         )
         total = main + tail
-        sum_m[pl.ds(c, TOKENS, stride=SHARE), :] = total[:, :128]
-        sum_t[pl.ds(c, TOKENS, stride=SHARE), :] = pad_lanes(total[:, 128:])
-
-    @pl.loop(0, PARTS)
-    def _(step):
-        part = other(step)
-        at = pl.multiple_of(part * ROWS * SHARE, ROWS * SHARE)
-        send2[part, 0:80] = sum_m[pl.ds(at, 80), :].astype(BF16)
-        rest = sum_t[pl.ds(at, 80), :][:, :TAIL]
-        packed = jnp.concatenate([rest[16 * t : 16 * t + 16] for t in range(4)], axis=1)
-        send2[part, 80:96] = packed.astype(BF16)
-        send2[part, 96:112] = pad_lanes(rest[64:80]).astype(BF16)
+        sum_m[at_l, :] = total[:, :128]
+        sum_t[at_l, :] = pad_lanes(total[:, 128:])
+
+    @pl.loop(0, NEAR)
+    def _(step):
+        slot = near(step)
+        at = pl.ds(pl.multiple_of(slot * ROWS * SHARE, ROWS * SHARE), ROWS * SHARE)
+        send2[slot, 0:ROWS] = sum_m[at, :].astype(BF16).reshape(ROWS, SHARE, 128)
+        rest = sum_t[at, :][:, :TAIL]
+        for tile in range(3):
+            parts = [rest[SHARE * i : SHARE * i + SHARE] for i in range(4 * tile, min(4 * tile + 4, ROWS))]
+            packed = jnp.concatenate(parts, axis=1)
+            if len(parts) < 4:
+                packed = pad_lanes(packed)
+            send2[slot, ROWS + tile] = packed.astype(BF16)
 
         @pl.when(step > 0)
         def _():
-            copy_to(1, send2.at[part], recv2, part).start()
-
-    recv2[me] = send2[me]
-
-    @pl.loop(0, PARTS)
-    def _(step):
-        source = other(step)
-
-        @pl.when(step > 0)
-        def _():
-            arrived(1, recv2, source).wait_recv()
-
-        recv2_f[source] = recv2[source].astype(F32)
+            sum_copy(slot).start()
+
+    recv2[place] = send2[place]
+
+    @pl.loop(1, NEAR)
+    def _(step):
+        arrived(1, recv2, near(step)).wait_recv()
 
     for i in range(ROWS):
-        summed[i, :, 0:128] = recv2_f[:, SHARE * i : SHARE * i + SHARE, :].reshape(WIDTH, 128)
-        row = 80 + SHARE * (i % 2) + (16 if i >= 8 else 0)
-        lane = TAIL * ((i // 2) % 4)
-        rest = recv2_f[:, row : row + SHARE, :].reshape(WIDTH, 128)
+        summed[i, :, 0:128] = recv2[:, i].astype(F32).reshape(WIDTH, 128)
+        lane = TAIL * (i % 4)
+        rest = recv2[:, ROWS + i // 4].astype(F32).reshape(WIDTH, 128)
         summed[i, :, 128:TOKENS] = rest[:, lane : lane + TAIL]
 
     high = bias_v[...].astype(BF16).astype(F32)
@@ -370,10 +408,11 @@
         )
     ).astype(BF16)
 
-    @pl.loop(1, PARTS)
-    def _(step):
-        part = other(step)
-        copy_to(2, send3, recv3, part).start()
+    bias_copy(across).start()
+
+    @pl.loop(1, NEAR)
+    def _(step):
+        bias_copy(first + near(step)).start()
 
     recv3[me] = send3[...]
 
@@ -383,8 +422,7 @@
     block = (lane >= channel * TOKENS) & (lane < channel * TOKENS + TOKENS)
     scale = (WIDTH // HEADS) ** (-0.5)
 
-    @pl.loop(0, ROWS)
-    def _(i):
+    def attention_inputs(i):
         mid_n = mid_norm[i]
         rest = jnp.dot(mid_n, att_proj[:, WIDTH:], preferred_element_type=F32)
         key[i] = rest[:, 0:WIDTH].astype(BF16)
@@ -393,6 +431,15 @@
         wide = dot(query_t, jnp.concatenate([mid_n] * HEADS, axis=0), NT)
         query[i] = jnp.where(block, wide * scale, 0.0).astype(BF16)
 
+    pl.loop(0, EARLY)(attention_inputs)
+    arrived(2, recv3, across).wait_recv()
+
+    @pl.loop(1, NEAR)
+    def _(step):
+        passed_copy(near(step)).start()
+
+    pl.loop(EARLY, ROWS)(attention_inputs)
+
     ids = lax.broadcasted_iota(jnp.int32, (16, TOKENS), 0)
     one_hot = jnp.where(ids == chain_v[...], 1.0, 0.0).astype(BF16)
     same = dot(one_hot, one_hot, TN)
@@ -402,7 +449,7 @@
     def _(step):
         source = other(step)
 
-        @pl.when(step > 0)
+        @pl.when((step > 0) & (step != NEAR))
         def _():
             arrived(2, recv3, source).wait_recv()
 
@@ -443,10 +490,17 @@
 
     @pl.loop(1, PARTS)
     def _(step):
-        part = other(step)
-        copy_to(0, send1.at[part], recv1, part).wait_send()
-        copy_to(1, send2.at[part], recv2, part).wait_send()
-        copy_to(2, send3, recv3, part).wait_send()
+        right_copy(other(step)).wait_send()
+
+    bias_copy(across).wait_send()
+
+    @pl.loop(1, NEAR)
+    def _(step):
+        slot = near(step)
+        left_copy(slot).wait_send()
+        sum_copy(slot).wait_send()
+        bias_copy(first + slot).wait_send()
+        passed_copy(slot).wait_send()
 
 
 def per_device_fused(
@@ -477,15 +531,18 @@
             pltpu.VMEM((4 * WIDTH, WIDTH), BF16),
             pltpu.VMEM(all_rows, BF16),
             pltpu.VMEM((ROWS, 2 * WIDTH, TAIL), F32),
-            pltpu.VMEM((PARTS, 13, 16, 128), BF16),
-            pltpu.VMEM((PARTS, 13, 16, 128), BF16),
-            pltpu.VMEM((TOKENS * 16, 128), F32),
-            pltpu.VMEM((TOKENS * 16, 128), F32),
+            pltpu.VMEM((NEAR, TILES, SHARE, 128), BF16),
+            pltpu.VMEM((NEAR, TILES, SHARE, 128), BF16),
+            pltpu.VMEM((NEAR, TILES, SHARE, 128), BF16),
+            pltpu.VMEM((PARTS, TILES, SHARE, 128), BF16),
+            pltpu.VMEM((TOKENS // 2 * SHARE, 128), F32),
+            pltpu.VMEM((TOKENS // 2 * SHARE, 128), F32),
             pltpu.VMEM((TOKENS * SHARE, 128), F32),
             pltpu.VMEM((TOKENS * SHARE, 128), F32),
-            pltpu.VMEM((PARTS, 112, 128), BF16),
-            pltpu.VMEM((PARTS, 112, 128), BF16),
-            pltpu.VMEM((PARTS, 112, 128), F32),
+            pltpu.VMEM((TOKENS // 2 * SHARE, 128), F32),
+            pltpu.VMEM((TOKENS // 2 * SHARE, 128), F32),
+            pltpu.VMEM((NEAR, TILES, SHARE, 128), BF16),
+            pltpu.VMEM((NEAR, TILES, SHARE, 128), BF16),
             pltpu.VMEM((ROWS, WIDTH, TOKENS), F32),
             pltpu.VMEM(all_rows, F32),
             pltpu.VMEM(all_rows, BF16),
@@ -500,8 +557,8 @@
             pltpu.VMEM(all_rows, BF16),
             pltpu.VMEM(all_rows, BF16),
             pltpu.VMEM(all_rows, F32),
-            pltpu.SemaphoreType.DMA((3, PARTS)),
-            pltpu.SemaphoreType.DMA((3, PARTS)),
+            pltpu.SemaphoreType.DMA((5, PARTS)),
+            pltpu.SemaphoreType.DMA((5, PARTS)),
             pltpu.SemaphoreType.DMA((10,)),
         ],
         compiler_params=pltpu.CompilerParams(

time: 60.4 us -> 60.3 us (level)
  no operation moved by 1% of the time
where the time goes in v4:
time: 60.3 us; the launch traced here: 60.1 us
  Pallas kernels  58.3 us (97%)
  local copies, waits for them, and re-layouts  1.78 us (3%)
    pallas_call x1, Pallas kernels, per_device_fused(): pl.pallas_call(fused_kernel, out_shape=jax.ShapeDtypeStruct(all_rows, BF1...  58.3 us
    unnamed x1, local copies, waits for them, and re-layouts  1.78 us

profile of v4, /device:TPU:0, one launch (start us, length us, event | category | flops | bytes accessed | tf_op | source)
XLA Modules:
  0.0 60.1 jit_solution(8229853343447544696)
XLA Ops:
  0.0 58.3 %shard_map.100 = bf16[10,160,128]{2,1,0:T(8,128)(2,1)} custom-call(bf16[10,160,128]{2,1,0:T(8,128)(2,1)} %refs_0_.1, bf16[128,512]{1,0:T(8,128)(2,1)} %refs_1_.1, s32[1,160]{1,0:T(1,128)} %bitcast.5, bf16[128,128]{1,0:T(8,128)(2,1)} %refs_3_.1, bf16[128,128]{1,0:T(8,128)(2,1)} %refs_4_.1, f32[4,128]{1,0:T(4,128)} %bitcast.4, bf16[128,512]{1,0:T(8,128)(2,1)} %refs_6_.1, ...), custom_call_target="tpu_custom_call" | custom-call | tf_op jit(solution)/shard_map/pallas_call | solution.py:524
  58.3 1.8 %copy.12 = bf16[10,160,128]{2,1,0:T(8,128)(2,1)} copy(bf16[10,160,128]{2,1,0:T(8,128)(2,1)} %shard_map.100) | data formatting | bytes 819200

commit v5 on v4

--- a/solution.py
+++ b/solution.py
@@ -266,32 +266,36 @@
     for fetch in fetches[:3]:
         fetch.wait()
 
-    proj_t[...] = tri_proj[...].astype(F32).T.astype(BF16)
+    turned = tri_proj[...].astype(F32).T
+    order = [turned[WIDTH * at : WIDTH * at + WIDTH] for at in (1, 3, 0, 2)]
+    proj_t[...] = jnp.concatenate(order, axis=0).astype(BF16)
     mask_row = mask_v[...].astype(F32)
     token = lax.broadcasted_iota(jnp.int32, (1, TOKENS), 1)
 
-    @pl.loop(0, ROWS)
+    def project(i, row, side, send):
+        weights = proj_t[2 * WIDTH * side : 2 * WIDTH * side + 2 * WIDTH]
+        projected = dot(weights, row, NT)
+        mine = jnp.where(token == me * ROWS + i, mask_row, 0.0)
+        weight = mask_row * jnp.sum(mine, axis=1, keepdims=True)
+        one = weight * jax.nn.sigmoid(projected[WIDTH:]) * projected[:WIDTH]
+        send[:, i] = one[:, :128].astype(BF16).reshape(NEAR, SHARE, 128)
+        tails[i] = one[:, 128:]
+
+    def pack_tails(send):
+        for tile in range(3):
+            parts = [tails[i] for i in range(4 * tile, min(4 * tile + 4, ROWS))]
+            packed = jnp.concatenate(parts, axis=1)
+            if len(parts) < 4:
+                packed = pad_lanes(packed)
+            send[:, ROWS + tile] = packed.astype(BF16).reshape(NEAR, SHARE, 128)
+
+    @pl.loop(0, ROWS, unroll=2)
     def _(i):
         row = norm(pair[i].astype(F32), 1)
         normed[i] = row
-        projected = dot(proj_t[...], row, NT)
-        mine = jnp.where(token == me * ROWS + i, mask_row, 0.0)
-        weight = mask_row * jnp.sum(mine, axis=1, keepdims=True)
-        both = weight * jax.nn.sigmoid(projected[2 * WIDTH :]) * projected[: 2 * WIDTH]
-        main = both[:, :128].astype(BF16)
-        send_l[:, i] = main[:WIDTH].reshape(NEAR, SHARE, 128)
-        send_r[:, i] = main[WIDTH:].reshape(NEAR, SHARE, 128)
-        tails[i] = both[:, 128:]
-
-    for tile in range(3):
-        parts = [tails[i] for i in range(4 * tile, min(4 * tile + 4, ROWS))]
-        packed = jnp.concatenate(parts, axis=1)
-        if len(parts) < 4:
-            packed = pad_lanes(packed)
-        packed = packed.astype(BF16)
-        send_l[:, ROWS + tile] = packed[:WIDTH].reshape(NEAR, SHARE, 128)
-        send_r[:, ROWS + tile] = packed[WIDTH:].reshape(NEAR, SHARE, 128)
-
+        project(i, row, 0, send_r)
+
+    pack_tails(send_r)
     pl.semaphore_wait(barrier, PARTS - 1)
 
     @pl.loop(0, NEAR)
@@ -301,6 +305,15 @@
     @pl.loop(1, NEAR)
     def _(step):
         right_copy(first + near(step)).start()
+
+    @pl.loop(0, ROWS, unroll=2)
+    def _(i):
+        project(i, normed[i], 1, send_l)
+
+    pack_tails(send_l)
+
+    @pl.loop(1, NEAR)
+    def _(step):
         left_copy(near(step)).start()
 
     recv_l[place] = send_l[place]
@@ -308,7 +321,7 @@
     for fetch in fetches[3:]:
         fetch.wait()
 
-    @pl.loop(0, ROWS)
+    @pl.loop(0, ROWS, unroll=5)
     def _(i):
         gate[i] = jax.nn.sigmoid(jnp.dot(normed[i], tri_gate[...], preferred_element_type=F32))
 
@@ -381,7 +394,7 @@
     none = jnp.zeros((HEADS, WIDTH), F32)
     bias_t = jnp.concatenate([high, none, bias_v[...] - high, none], axis=0).astype(BF16)
 
-    @pl.loop(0, ROWS // 2)
+    @pl.loop(0, ROWS // 2, unroll=5)
     def _(pair_at):
         biases = []
         for half in range(2):
@@ -431,14 +444,14 @@
         wide = dot(query_t, jnp.concatenate([mid_n] * HEADS, axis=0), NT)
         query[i] = jnp.where(block, wide * scale, 0.0).astype(BF16)
 
-    pl.loop(0, EARLY)(attention_inputs)
+    pl.loop(0, EARLY, unroll=5)(attention_inputs)
     arrived(2, recv3, across).wait_recv()
 
     @pl.loop(1, NEAR)
     def _(step):
         passed_copy(near(step)).start()
 
-    pl.loop(EARLY, ROWS)(attention_inputs)
+    pl.loop(EARLY, ROWS, unroll=5)(attention_inputs)
 
     ids = lax.broadcasted_iota(jnp.int32, (16, TOKENS), 0)
     one_hot = jnp.where(ids == chain_v[...], 1.0, 0.0).astype(BF16)
@@ -474,7 +487,7 @@
 
     head_of = lax.broadcasted_iota(jnp.int32, (TOKENS, WIDTH), 1) // (WIDTH // HEADS)
 
-    @pl.loop(0, ROWS)
+    @pl.loop(0, ROWS, unroll=5)
     def _(i):
         scores = jnp.dot(key[i], query[i], preferred_element_type=F32) + logit[...]
         top = jnp.max(scores, axis=0, keepdims=True)
@@ -530,7 +543,7 @@
         + [
             pltpu.VMEM((4 * WIDTH, WIDTH), BF16),
             pltpu.VMEM(all_rows, BF16),
-            pltpu.VMEM((ROWS, 2 * WIDTH, TAIL), F32),
+            pltpu.VMEM((ROWS, WIDTH, TAIL), F32),
             pltpu.VMEM((NEAR, TILES, SHARE, 128), BF16),
             pltpu.VMEM((NEAR, TILES, SHARE, 128), BF16),
             pltpu.VMEM((NEAR, TILES, SHARE, 128), BF16),

time: 60.3 us -> 55.9 us (0.927)
  Pallas kernels: 58.3 us -> 54 us
    pallas_call x1, Pallas kernels: 58.3 us -> 54 us  [per_device_fused(): pl.pallas_call(fused_kernel, out_shape=jax.ShapeDtypeStruct(all_rows, BF1...]
where the time goes in v5:
time: 55.9 us; the launch traced here: 55.8 us
  Pallas kernels  54 us (97%)
  local copies, waits for them, and re-layouts  1.78 us (3%)
    pallas_call x1, Pallas kernels, per_device_fused(): pl.pallas_call(fused_kernel, out_shape=jax.ShapeDtypeStruct(all_rows, BF1...  54 us
    unnamed x1, local copies, waits for them, and re-layouts  1.78 us

profile of v5, /device:TPU:0, one launch (start us, length us, event | category | flops | bytes accessed | tf_op | source)
XLA Modules:
  0.0 55.8 jit_solution(9581602682352165398)
XLA Ops:
  0.0 54.0 %shard_map.100 = bf16[10,160,128]{2,1,0:T(8,128)(2,1)} custom-call(bf16[10,160,128]{2,1,0:T(8,128)(2,1)} %refs_0_.1, bf16[128,512]{1,0:T(8,128)(2,1)} %refs_1_.1, s32[1,160]{1,0:T(1,128)} %bitcast.5, bf16[128,128]{1,0:T(8,128)(2,1)} %refs_3_.1, bf16[128,128]{1,0:T(8,128)(2,1)} %refs_4_.1, f32[4,128]{1,0:T(4,128)} %bitcast.4, bf16[128,512]{1,0:T(8,128)(2,1)} %refs_6_.1, ...), custom_call_target="tpu_custom_call" | custom-call | tf_op jit(solution)/shard_map/pallas_call | solution.py:537
  54.0 1.8 %copy.12 = bf16[10,160,128]{2,1,0:T(8,128)(2,1)} copy(bf16[10,160,128]{2,1,0:T(8,128)(2,1)} %shard_map.100) | data formatting | bytes 819200

commit v6 on v5

--- a/solution.py
+++ b/solution.py
@@ -206,6 +206,7 @@
     att_gate,
     sends,
     recvs,
+    stores,
 ):
     me = lax.axis_index("row")
 
@@ -485,6 +486,9 @@
     logit[0:128, :] = jnp.concatenate(mains, axis=0).T
     logit[128:TOKENS, :] = jnp.concatenate(rests, axis=0).T[0:TAIL]
 
+    def row_out(i):
+        return pltpu.make_async_copy(mid.at[i], out.at[i], stores.at[i])
+
     head_of = lax.broadcasted_iota(jnp.int32, (TOKENS, WIDTH), 1) // (WIDTH // HEADS)
 
     @pl.loop(0, ROWS, unroll=5)
@@ -499,13 +503,18 @@
             mixed = jnp.where(head_of == h, mixes[h * TOKENS : (h + 1) * TOKENS], mixed)
         gated = (att_gate[i] * mixed).astype(BF16)
         added = jnp.dot(gated, att_out[...], preferred_element_type=F32)
-        out[i] = (mid[i].astype(F32) + added).astype(BF16)
+        mid[i] = (mid[i].astype(F32) + added).astype(BF16)
+        row_out(i).start()
 
     @pl.loop(1, PARTS)
     def _(step):
         right_copy(other(step)).wait_send()
 
     bias_copy(across).wait_send()
+
+    @pl.loop(0, ROWS)
+    def _(i):
+        row_out(i).wait()
 
     @pl.loop(1, NEAR)
     def _(step):
@@ -520,7 +529,6 @@
     pair, mask, chain, tri_proj, tri_gate, tri_out, att_proj, att_bias, same_chain, att_out
 ):
     hbm = pl.BlockSpec(memory_space=pltpu.HBM)
-    vmem = pl.BlockSpec(memory_space=pltpu.VMEM)
     all_rows = (ROWS, TOKENS, WIDTH)
     inputs = (
         pair,
@@ -538,7 +546,7 @@
         fused_kernel,
         out_shape=jax.ShapeDtypeStruct(all_rows, BF16),
         in_specs=[hbm] * 10,
-        out_specs=vmem,
+        out_specs=hbm,
         scratch_shapes=[pltpu.VMEM(each.shape, each.dtype) for each in inputs]
         + [
             pltpu.VMEM((4 * WIDTH, WIDTH), BF16),
@@ -572,6 +580,7 @@
             pltpu.VMEM(all_rows, F32),
             pltpu.SemaphoreType.DMA((5, PARTS)),
             pltpu.SemaphoreType.DMA((5, PARTS)),
+            pltpu.SemaphoreType.DMA((ROWS,)),
             pltpu.SemaphoreType.DMA((10,)),
         ],
         compiler_params=pltpu.CompilerParams(

time: 55.9 us -> 55.7 us (level)
  no operation moved by 1% of the time
where the time goes in v6:
time: 55.7 us; the launch traced here: 55.6 us
  Pallas kernels  53.8 us (97%)
  local copies, waits for them, and re-layouts  1.78 us (3%)
    pallas_call x1, Pallas kernels, per_device_fused(): pl.pallas_call(fused_kernel, out_shape=jax.ShapeDtypeStruct(all_rows, BF1...  53.8 us
    unnamed x1, local copies, waits for them, and re-layouts  1.78 us

profile of v6, /device:TPU:0, one launch (start us, length us, event | category | flops | bytes accessed | tf_op | source)
XLA Modules:
  0.0 55.6 jit_solution(15535831608352767073)
XLA Ops:
  0.0 53.8 %shard_map.100 = bf16[10,160,128]{2,1,0:T(8,128)(2,1)} custom-call(bf16[10,160,128]{2,1,0:T(8,128)(2,1)} %refs_0_.1, bf16[128,512]{1,0:T(8,128)(2,1)} %refs_1_.1, s32[1,160]{1,0:T(1,128)} %bitcast.5, bf16[128,128]{1,0:T(8,128)(2,1)} %refs_3_.1, bf16[128,128]{1,0:T(8,128)(2,1)} %refs_4_.1, f32[4,128]{1,0:T(4,128)} %bitcast.4, bf16[128,512]{1,0:T(8,128)(2,1)} %refs_6_.1, ...), custom_call_target="tpu_custom_call" | custom-call | tf_op jit(solution)/shard_map/pallas_call | solution.py:545
  53.8 1.8 %copy.12 = bf16[10,160,128]{2,1,0:T(8,128)(2,1)} copy(bf16[10,160,128]{2,1,0:T(8,128)(2,1)} %shard_map.100) | data formatting | bytes 819200

commit v7 on v6

--- a/solution.py
+++ b/solution.py
@@ -362,7 +362,7 @@
         sum_m[at_l, :] = total[:, :128]
         sum_t[at_l, :] = pad_lanes(total[:, 128:])
 
-    @pl.loop(0, NEAR)
+    @pl.loop(1, NEAR + 1)
     def _(step):
         slot = near(step)
         at = pl.ds(pl.multiple_of(slot * ROWS * SHARE, ROWS * SHARE), ROWS * SHARE)
@@ -375,7 +375,7 @@
                 packed = pad_lanes(packed)
             send2[slot, ROWS + tile] = packed.astype(BF16)
 
-        @pl.when(step > 0)
+        @pl.when(step < NEAR)
         def _():
             sum_copy(slot).start()
 
@@ -467,12 +467,13 @@
         def _():
             arrived(2, recv3, source).wait_recv()
 
-        at = pl.multiple_of(source * 40, 8)
+    for source in range(PARTS):
+        at = source * ROWS * HEADS
         got = recv3[source].astype(F32)
-        bias_m[pl.ds(at, 40), :] = got[0:40]
+        bias_m[at : at + 40, :] = got[0:40]
         for t in range(3):
             size = 16 if t < 2 else 8
-            bias_tl[pl.ds(pl.multiple_of(at + 16 * t, 8), size), 0:TAIL] = got[
+            bias_tl[at + 16 * t : at + 16 * t + size, 0:TAIL] = got[
                 48 : 48 + size, TAIL * t : TAIL * t + TAIL
             ]
 

time: 55.7 us -> 55.6 us (level)
  no operation moved by 1% of the time
where the time goes in v7:
time: 55.6 us; the launch traced here: 55.4 us
  Pallas kernels  53.6 us (96%)
  local copies, waits for them, and re-layouts  1.78 us (3%)
    pallas_call x1, Pallas kernels, per_device_fused(): pl.pallas_call(fused_kernel, out_shape=jax.ShapeDtypeStruct(all_rows, BF1...  53.6 us
    unnamed x1, local copies, waits for them, and re-layouts  1.78 us

profile of v7, /device:TPU:0, one launch (start us, length us, event | category | flops | bytes accessed | tf_op | source)
XLA Modules:
  0.0 55.4 jit_solution(11881776131388025425)
XLA Ops:
  0.0 53.6 %shard_map.100 = bf16[10,160,128]{2,1,0:T(8,128)(2,1)} custom-call(bf16[10,160,128]{2,1,0:T(8,128)(2,1)} %refs_0_.1, bf16[128,512]{1,0:T(8,128)(2,1)} %refs_1_.1, s32[1,160]{1,0:T(1,128)} %bitcast.5, bf16[128,128]{1,0:T(8,128)(2,1)} %refs_3_.1, bf16[128,128]{1,0:T(8,128)(2,1)} %refs_4_.1, f32[4,128]{1,0:T(4,128)} %bitcast.4, bf16[128,512]{1,0:T(8,128)(2,1)} %refs_6_.1, ...), custom_call_target="tpu_custom_call" | custom-call | tf_op jit(solution)/shard_map/pallas_call | solution.py:546
  53.7 1.8 %copy.12 = bf16[10,160,128]{2,1,0:T(8,128)(2,1)} copy(bf16[10,160,128]{2,1,0:T(8,128)(2,1)} %shard_map.100) | data formatting | bytes 819200
